TPU v7x, 32 devices: a whole 2x2x4 slice. The times are simulated.
32 devices in a mesh: section: 4 (over y, core), gy: 4 (over z), gx: 2 (over x).
Axes of the slice: x: 2, y: 2, z: 4, core: 2. Of those that a mesh axis runs over, the one named last changes fastest.
Arguments:
- fields: float32 [4, 15, 16, 32, 512], P('section', None, None, 'gy', 'gx'), may hold values from -2 to 2, as said below
- sea_mask: int32 [96, 512], replicated, may hold values 0 or 1
- bottom: int32 [96, 512], replicated, may hold values from 2 to 16
- reaction: float32 [15, 15], replicated, may hold values from -1.5 to 1.5
- growth: float32 [15], replicated, may hold values from 0.3 to 3
Outputs:
- advanced: float32 [4, 15, 16, 32, 512], P('section', None, None, 'gy', 'gx')
Inputs may be any that keep to these rules, and one draw needn't show every extreme that they name: `fields`: in slab 0 the velocity channels lie within -1 to 1 and the turbulent energy channels within 0 to 1.5; tracer slabs are positive.
All inputs are finite; a program needn't handle non-finite values.
Results may differ from a plain program's by a relative error of at most 0.0003.
Values sent between devices are 32-bit elements; how exact they have to be, the bound alone decides.
A program may use at most 128 MiB of HBM per device.

v0:
```python
import functools

import jax
import jax.numpy as jnp
from jax import lax
from jax.experimental import pallas as pl
from jax.experimental.pallas import tpu as pltpu
from jax.sharding import PartitionSpec as P

STEPS = 2

TIME_INCREMENT = 0.2
CORIOLIS = 0.5
PRESSURE = 0.5
VISCOSITY = 0.15
DRAG_RATE = 0.1
DIFFUSION_RATE = 0.15
THERMAL_FORCING = 3.0
SHEAR_GAIN = 0.5
DISSIPATION = 0.5
KAPPA_BASE = 0.05
KAPPA_GAIN = 0.15
EXPANSION = 0.2
CONTRACTION = 0.8
WATER_SHADE = 0.05
CHLOROPHYLL_SHADE = 0.1
HALF_SAT = 0.5

MESH = pl.DeviceIdType.MESH
LANES = 128
SUBS = 8
KB = 4
SLOT_FIELD = (0, 1, 4, 2, 3)
U, V, E, T, S = range(5)


def minmod(a, b):
    return jnp.minimum(jnp.maximum(a, jnp.minimum(b, 0.0)), jnp.maximum(b, 0.0))


def iota(shape, dim):
    return lax.broadcasted_iota(jnp.int32, shape, dim)


def ahead(x, axis):
    return pltpu.roll(x, x.shape[axis] - 1, axis)


def behind(x, axis):
    return pltpu.roll(x, 1, axis)


def kernel(
    row_tiles, col_tiles,
    fields, depth, reaction, growth, out,
    state, base, coef_c, coef_r, coef_v, uptake, sun,
    col_out, col_in, row_out, row_in, orow_out, orow_in,
    flow_in, fcol_in, frow_in, heat_out, heat_in,
    send_sem, recv_sem,
):
    channels, levels, rows, cols = fields.shape[1:]
    section = lax.axis_index("section")
    g = lax.axis_index("gy")
    x = lax.axis_index("gx")
    is_ocean = section == 0
    is_tracer = section != 0
    even = lax.rem(g, 2) == 0
    third = jnp.maximum(jnp.where(even, section - 1, 3 - section), 0)
    band = 3 * g + third
    bands = 3 * row_tiles
    wide = cols + LANES

    def band_device(b):
        tile = b // 3
        t = lax.rem(b, 3)
        return (jnp.where(lax.rem(tile, 2) == 0, t + 1, 3 - t), tile, x)

    def own_tracer(t, col):
        return (jnp.where(even, t + 1, 3 - t), g, col)

    has_w, has_e = x > 0, x < col_tiles - 1
    has_s, has_n = g > 0, g < row_tiles - 1
    pairs = [(has_w, (section, g, x - 1)), (has_e, (section, g, x + 1))]
    pairs += [(is_ocean & has_s, (0, g - 1, x)), (is_ocean & has_n, (0, g + 1, x))]
    for t in range(3):
        pairs.append((is_ocean, own_tracer(t, x)))
        pairs.append((is_ocean & has_w, own_tracer(t, x - 1)))
        pairs.append((is_ocean & has_e, own_tracer(t, x + 1)))
    pairs.append((is_ocean & has_s, band_device(jnp.maximum(3 * g - 1, 0))))
    pairs.append((is_ocean & has_n, band_device(3 * g + 3)))
    has_lo, has_hi = band > 0, band < bands - 1
    pairs.append((is_tracer & has_lo, band_device(jnp.maximum(band - 1, 0))))
    pairs.append((is_tracer & has_hi, band_device(band + 1)))
    pairs.append((is_tracer, (0, g, x)))
    pairs.append((is_tracer & has_w, (0, g, x - 1)))
    pairs.append((is_tracer & has_e, (0, g, x + 1)))
    pairs.append((is_tracer & has_s & (third == 0), (0, g - 1, x)))
    pairs.append((is_tracer & has_n & (third == 2), (0, g + 1, x)))
    barrier = pltpu.get_barrier_semaphore()
    count = jnp.int32(0)
    for there, device in pairs:
        @pl.when(there)
        def _(device=device):
            pl.semaphore_signal(barrier, inc=1, device_id=device, device_id_type=MESH)
        count = count + there.astype(jnp.int32)

    def copy(src, dst, step, sent, received, device):
        return pltpu.make_async_remote_copy(
            src_ref=src, dst_ref=dst, send_sem=send_sem.at[step, sent],
            recv_sem=recv_sem.at[step, received], device_id=device, device_id_type=MESH,
        )

    def common_sends(step):
        return [
            (has_w, copy(col_out.at[step, 0], col_in.at[step, 1], step, 0, 1, (section, g, x - 1))),
            (has_e, copy(col_out.at[step, 1], col_in.at[step, 0], step, 1, 0, (section, g, x + 1))),
        ]

    def tracer_row_sends(step):
        return [
            (has_lo, copy(row_out.at[step, 0], row_in.at[step, 1], step, 2, 3, band_device(jnp.maximum(band - 1, 0)))),
            (has_hi, copy(row_out.at[step, 1], row_in.at[step, 0], step, 3, 2, band_device(band + 1))),
        ]

    def heat_send(step):
        return copy(heat_out.at[step], heat_in.at[step, third], step, 4, 9 + third, (0, g, x))

    def flow_sends(step):
        return [
            (is_ocean, copy(state.at[step, pl.ds(5 * t, 3), pl.ds(1, levels)], flow_in.at[step], step, 5 + t, 4, own_tracer(t, x)))
            for t in range(3)
        ]

    def ocean_edge_sends(step):
        found = []
        for t in range(3):
            cols_of = pl.ds(5 * t, 5)
            found.append((has_w, copy(col_out.at[step, 0, cols_of], fcol_in.at[step, 1], step, 8 + t, 6, own_tracer(t, x - 1))))
            found.append((has_e, copy(col_out.at[step, 1, cols_of], fcol_in.at[step, 0], step, 11 + t, 5, own_tracer(t, x + 1))))
            mine = 3 * g + t
            found.append((mine > 0, copy(orow_out.at[step, 0, pl.ds(5 * t + V, 2)], frow_in.at[step, 1], step, 14 + t, 8, band_device(jnp.maximum(mine - 1, 0)))))
            found.append((mine < bands - 1, copy(orow_out.at[step, 1, pl.ds(5 * t + V, 2)], frow_in.at[step, 0], step, 17 + t, 7, band_device(mine + 1))))
        found.append((has_s, copy(orow_out.at[step, 0, pl.ds(0, 5)], orow_in.at[step, 1], step, 2, 3, (0, g - 1, x))))
        found.append((has_n, copy(orow_out.at[step, 1, pl.ds(10, 5)], orow_in.at[step, 0], step, 3, 2, (0, g + 1, x))))
        return found

    def start(sends):
        for there, one in sends:
            @pl.when(there)
            def _(one=one):
                one.start()

    def finish(sends):
        for there, one in sends:
            @pl.when(there)
            def _(one=one):
                one.wait_send()

    def arrived(there, dst, step, received):
        @pl.when(there)
        def _():
            copy(dst, dst, step, 0, received, (section, g, x)).wait_recv()

    lane = iota((rows, LANES), 1)
    sub_full = iota((SUBS, cols), 0)
    for step in range(STEPS):
        for side, there in ((0, has_w), (1, has_e)):
            @pl.when(jnp.logical_not(there))
            def _(step=step, side=side):
                col_in[step, side] = jnp.zeros(col_in.shape[2:], jnp.float32)
                fcol_in[step, side] = jnp.zeros(fcol_in.shape[2:], jnp.float32)
        for side, there, ocean_there in ((0, has_lo, has_s), (1, has_hi, has_n)):
            @pl.when(is_tracer & jnp.logical_not(there))
            def _(step=step, side=side):
                row_in[step, side] = jnp.zeros(row_in.shape[2:], jnp.float32)
                frow_in[step, side] = jnp.zeros(frow_in.shape[2:], jnp.float32)
            @pl.when(is_ocean & jnp.logical_not(ocean_there))
            def _(step=step, side=side):
                orow_in[step, side] = jnp.zeros(orow_in.shape[2:], jnp.float32)

    def pack_columns(step):
        def one(c, carry):
            low = jnp.zeros((rows, LANES), jnp.float32)
            high = low
            for k in range(levels):
                mine = (lane >= 2 * k) & (lane < 2 * k + 2)
                left = state[step, c, k + 1, :, :LANES]
                right = state[step, c, k + 1, :, cols - LANES:]
                if k:
                    left = pltpu.roll(left, 2 * k, 1)
                low = jnp.where(mine, left, low)
                high = jnp.where(mine, pltpu.roll(right, (2 * k + 2) % LANES, 1), high)
            col_out[step, 0, c] = low
            col_out[step, 1, c] = high
            return carry
        lax.fori_loop(0, channels, one, 0)

    def column_halo(low, high, k):
        east = high if k == 0 else pltpu.roll(high, LANES - 2 * k, 1)
        west = pltpu.roll(low, (LANES - 2 - 2 * k) % LANES, 1)
        return jnp.where(lane < LANES // 2, east, west)

    def widen(value, low, high, k):
        return jnp.concatenate([value, column_halo(low, high, k)], axis=-1)

    def depth_views(t):
        base_row = pl.multiple_of(rows + rows * t, rows)
        row = pl.ds(base_row, rows)
        middle = depth[row, LANES:LANES + cols]
        halo = jnp.where(lane < LANES // 2, depth[row, LANES + cols:], depth[row, :LANES])
        across = jnp.concatenate([middle, halo], axis=-1)
        above = depth[pl.ds(pl.multiple_of(base_row + rows, rows), rows), LANES:LANES + cols]
        below = depth[pl.ds(pl.multiple_of(base_row - rows, rows), rows), LANES:LANES + cols]
        along = jnp.concatenate([middle, jnp.where(sub_full < SUBS // 2, above, below)], axis=0)
        return middle, across, along

    def tracer():
        middle, across, along = depth_views(third)
        across_next = ahead(across, 1)
        along_next = ahead(along, 0)
        both_c = jnp.minimum(across, across_next)
        both_r = jnp.minimum(along, along_next)

        def load(c, carry):
            state[0, c, pl.ds(1, levels)] = fields[0, c]
            for slot in range(2):
                state[slot, c, 0] = jnp.zeros((rows, cols), jnp.float32)
                state[slot, c, levels + 1] = jnp.zeros((rows, cols), jnp.float32)
            return carry
        lax.fori_loop(0, channels, load, 0)

        for step in range(STEPS):
            last = step == STEPS - 1

            def pack_rows(c, carry):
                for k in range(levels):
                    row_out[step, 0, c, 2 * k:2 * k + 2] = state[step, c, k + 1, 0:2]
                    row_out[step, 1, c, 2 * k:2 * k + 2] = state[step, c, k + 1, rows - 2:rows]
                return carry
            lax.fori_loop(0, channels, pack_rows, 0)
            if step == 0:
                pl.semaphore_wait(barrier, count)
            start(tracer_row_sends(step))
            optical = jnp.zeros((rows, cols), jnp.float32)
            for k in range(levels):
                chlorophyll = jnp.maximum(state[step, 2, k + 1], 0.0)
                light = jnp.exp(-optical)
                heat_out[step, k] = CHLOROPHYLL_SHADE * chlorophyll * light
                optical = optical + (WATER_SHADE + CHLOROPHYLL_SHADE * chlorophyll)
                nutrient = jnp.maximum(state[step, 0, k + 1], 0.0)
                uptake[k] = nutrient / (nutrient + HALF_SAT) * light * TIME_INCREMENT
            heat_send(step).start()
            pack_columns(step)
            start(common_sends(step))

            def react(k, carry):
                values = [state[step, c, k + 1] for c in range(channels)]
                growing = [
                    growth[d] * (jnp.maximum(values[d], 0.0) * uptake[k]) for d in range(channels)
                ]
                for c in range(channels):
                    total = values[c]
                    for d in range(channels):
                        total = total + reaction[c, d] * growing[d]
                    base[c, k] = total
                return carry
            lax.fori_loop(0, levels, react, 0)

            arrived(is_tracer, flow_in.at[step], step, 4)
            arrived(has_w, fcol_in.at[step, 0], step, 5)
            arrived(has_e, fcol_in.at[step, 1], step, 6)
            arrived(has_lo, frow_in.at[step, 0], step, 7)
            arrived(has_hi, frow_in.at[step, 1], step, 8)
            zero = jnp.zeros((rows, cols), jnp.float32)
            coef_v[0] = zero
            coef_v[levels] = zero
            for k in range(levels):
                speed = widen(flow_in[step, U, k], fcol_in[step, 0, U], fcol_in[step, 1, U], k)
                kappa = KAPPA_BASE + KAPPA_GAIN * widen(
                    flow_in[step, E, k], fcol_in[step, 0, E], fcol_in[step, 1, E], k
                )
                opened = jnp.where(k < both_c, TIME_INCREMENT, 0.0)
                flow = speed * opened
                coef_c[0, k] = jnp.maximum(flow, 0.0)
                coef_c[1, k] = jnp.minimum(flow, 0.0)
                coef_c[2, k] = 0.5 * (kappa + ahead(kappa, 1)) * opened
                low_v = jnp.broadcast_to(frow_in[step, 0, 0, k:k + 1], (rows, cols))
                low_e = jnp.broadcast_to(frow_in[step, 0, 1, k:k + 1], (rows, cols))
                high_e = jnp.broadcast_to(frow_in[step, 1, 1, k:k + 1], (rows, cols))
                speed = jnp.concatenate([flow_in[step, V, k], low_v], axis=0)
                kappa = KAPPA_BASE + KAPPA_GAIN * jnp.concatenate(
                    [flow_in[step, E, k], jnp.where(sub_full < SUBS // 2, high_e, low_e)], axis=0
                )
                opened = jnp.where(k < both_r, TIME_INCREMENT, 0.0)
                flow = speed * opened
                coef_r[0, k] = jnp.maximum(flow, 0.0)
                coef_r[1, k] = jnp.minimum(flow, 0.0)
                coef_r[2, k] = 0.5 * (kappa + ahead(kappa, 0)) * opened
                if k:
                    mean = KAPPA_BASE + 0.5 * KAPPA_GAIN * (flow_in[step, E, k - 1] + flow_in[step, E, k])
                    coef_v[k] = mean * jnp.where(k < middle, TIME_INCREMENT, 0.0)

            arrived(has_w, col_in.at[step, 0], step, 0)
            arrived(has_e, col_in.at[step, 1], step, 1)
            arrived(has_lo, row_in.at[step, 0], step, 2)
            arrived(has_hi, row_in.at[step, 1], step, 3)

            def fluxes(q, coefs, k0, axis):
                window = pl.ds(k0, KB)
                change = ahead(q, axis) - q
                half = 0.5 * minmod(change, behind(change, axis))
                flux = (
                    coefs[0, window] * (q + half)
                    + coefs[1, window] * ahead(q - half, axis)
                    - coefs[2, window] * change
                )
                return behind(flux, axis) - flux

            def advance(c, carry):
                low_c, high_c = col_in[step, 0, c], col_in[step, 1, c]
                for k0 in range(0, levels, KB):
                    q = state[step, c, pl.ds(k0 + 1, KB)]
                    halo = jnp.stack([column_halo(low_c, high_c, k0 + j) for j in range(KB)])
                    total = base[c, pl.ds(k0, KB)]
                    total = total + fluxes(jnp.concatenate([q, halo], axis=2), coef_c, k0, 2)[:, :, :cols]
                    low_r = row_in[step, 0, c, pl.ds(2 * k0, 2 * KB)]
                    high_r = row_in[step, 1, c, pl.ds(2 * k0, 2 * KB)]
                    halo = jnp.stack([
                        jnp.where(
                            sub_full < SUBS // 2,
                            pltpu.roll(high_r, SUBS - 2 * j, 0) if j else high_r,
                            pltpu.roll(low_r, SUBS - 2 - 2 * j, 0) if j < KB - 1 else low_r,
                        )
                        for j in range(KB)
                    ])
                    total = total + fluxes(jnp.concatenate([q, halo], axis=1), coef_r, k0, 1)[:, :rows]
                    up = coef_v[pl.ds(k0 + 1, KB)] * (state[step, c, pl.ds(k0 + 2, KB)] - q)
                    down = coef_v[pl.ds(k0, KB)] * (q - state[step, c, pl.ds(k0, KB)])
                    total = total + (up - down)
                    fresh = jnp.stack([
                        jnp.where(k0 + j < middle, total[j], 0.0) for j in range(KB)
                    ])
                    if last:
                        out[0, c, pl.ds(k0, KB)] = fresh
                    else:
                        state[step + 1, c, pl.ds(k0 + 1, KB)] = fresh
                return carry
            lax.fori_loop(0, channels, advance, 0)

        for step in range(STEPS):
            finish(tracer_row_sends(step) + common_sends(step))
            heat_send(step).wait_send()

    def ocean():
        def load(t, carry):
            for slot in range(5):
                state[0, 5 * t + slot, pl.ds(1, levels)] = fields[0, 3 * SLOT_FIELD[slot] + t]
                for step in range(2):
                    state[step, 5 * t + slot, levels + 1] = jnp.zeros((rows, cols), jnp.float32)
            return carry
        lax.fori_loop(0, 3, load, 0)
        views = []
        for t in range(3):
            middle, across, along = depth_views(t)
            views.append((
                middle,
                ahead(across, 1)[:, :cols], behind(across, 1)[:, :cols],
                ahead(along, 0)[:rows], behind(along, 0)[:rows],
            ))

        for step in range(STEPS):
            last = step == STEPS - 1
            if step == 0:
                pl.semaphore_wait(barrier, count)
                start(flow_sends(step))

            def pack_rows(c, carry):
                for k in range(levels):
                    orow_out[step, 0, c, k:k + 1] = state[step, c, k + 1, 0:1]
                    orow_out[step, 1, c, k:k + 1] = state[step, c, k + 1, rows - 1:rows]
                return carry
            lax.fori_loop(0, channels, pack_rows, 0)
            pack_columns(step)
            start(ocean_edge_sends(step))
            start(common_sends(step))
            arrived(has_w, col_in.at[step, 0], step, 0)
            arrived(has_e, col_in.at[step, 1], step, 1)
            arrived(has_s, orow_in.at[step, 0], step, 2)
            arrived(has_n, orow_in.at[step, 1], step, 3)

            def store(t, slot, k, value):
                if last:
                    out[0, 3 * SLOT_FIELD[slot] + t, k] = value
                else:
                    state[step + 1, 5 * t + slot, k + 1] = value

            def level(k, carry):
                for t in range(3):
                    middle, east_d, west_d, north_d, south_d = views[t]
                    m = [
                        jnp.where(k < d, 1.0, 0.0)
                        for d in (middle, east_d, west_d, north_d, south_d)
                    ]
                    centre, steps = {}, {}
                    for slot in (U, V, T, S):
                        c = 5 * t + slot
                        value = state[step, c, k + 1]
                        low, high = col_in[step, 0, c], col_in[step, 1, c]
                        east = pltpu.roll(high, lax.rem(LANES - 2 * k, LANES), 1)
                        west = pltpu.roll(low, lax.rem(2 * LANES - 2 - 2 * k, LANES), 1)
                        ext = jnp.concatenate(
                            [value, jnp.where(lane < LANES // 2, east, west)], axis=-1
                        )
                        if t == 2:
                            top = orow_in[step, 1, slot, pl.ds(k, 1)]
                        else:
                            top = state[step, c + 5, k + 1, 0:1]
                        if t == 0:
                            bottom_row = orow_in[step, 0, slot, pl.ds(k, 1)]
                        else:
                            bottom_row = state[step, c - 5, k + 1, rows - 1:rows]
                        north = jnp.where(
                            sub_full == rows - 1, jnp.broadcast_to(top, (rows, cols)), ahead(value, 0)
                        )
                        south = jnp.where(
                            sub_full == 0, jnp.broadcast_to(bottom_row, (rows, cols)), behind(value, 0)
                        )
                        centre[slot] = value
                        steps[slot] = [
                            m[1] * (ahead(ext, 1)[:, :cols] - value),
                            m[2] * (behind(ext, 1)[:, :cols] - value),
                            m[3] * (north - value),
                            m[4] * (south - value),
                        ]
                    lap = {s: (v[0] + v[1] + v[2] + v[3]) * m[0] for s, v in steps.items()}
                    rho = [CONTRACTION * a - EXPANSION * b for a, b in zip(steps[S], steps[T])]
                    grad_x = 0.5 * (rho[0] - rho[1])
                    grad_y = 0.5 * (rho[2] - rho[3])
                    u, v = centre[U], centre[V]
                    energy = state[step, 5 * t + E, k + 1]
                    du = state[step, 5 * t + U, k + 2] - u
                    dv = state[step, 5 * t + V, k + 2] - v
                    shear = jnp.where(k + 1 < middle, du * du + dv * dv, 0.0)
                    store(t, U, k, m[0] * (u + TIME_INCREMENT * (
                        CORIOLIS * v - PRESSURE * grad_x + VISCOSITY * lap[U] - DRAG_RATE * u)))
                    store(t, V, k, m[0] * (v + TIME_INCREMENT * (
                        -CORIOLIS * u - PRESSURE * grad_y + VISCOSITY * lap[V] - DRAG_RATE * v)))
                    store(t, E, k, m[0] * (energy + TIME_INCREMENT * (
                        SHEAR_GAIN * shear - DISSIPATION * energy)))
                    store(t, T, k, m[0] * (centre[T] + TIME_INCREMENT * DIFFUSION_RATE * lap[T]))
                    store(t, S, k, m[0] * (centre[S] + TIME_INCREMENT * DIFFUSION_RATE * lap[S]))
                return carry
            lax.fori_loop(0, levels, level, 0)
            if not last:
                start(flow_sends(step + 1))
            for t in range(3):
                arrived(is_ocean, heat_in.at[step, t], step, 9 + t)

            def warm(k, carry):
                for t in range(3):
                    heat = jnp.where(
                        k < views[t][0], TIME_INCREMENT * THERMAL_FORCING * heat_in[step, t, k], 0.0
                    )
                    if last:
                        out[0, 3 * SLOT_FIELD[T] + t, k] = out[0, 3 * SLOT_FIELD[T] + t, k] + heat
                    else:
                        state[step + 1, 5 * t + T, k + 1] = state[step + 1, 5 * t + T, k + 1] + heat
                return carry
            lax.fori_loop(0, levels, warm, 0)

        for step in range(STEPS):
            finish(flow_sends(step) + ocean_edge_sends(step) + common_sends(step))

    pl.when(is_tracer)(tracer)
    pl.when(is_ocean)(ocean)


def on_device(fields, sea_mask, bottom, reaction, growth):
    _, channels, levels, rows, cols = fields.shape
    row_tiles, col_tiles = lax.axis_size("gy"), lax.axis_size("gx")
    depth = jnp.where(sea_mask == 1, bottom, 0)
    depth = jnp.pad(depth, ((rows, rows), (LANES, LANES)))
    depth = lax.dynamic_slice(
        depth,
        (lax.axis_index("gy") * 3 * rows, lax.axis_index("gx") * cols),
        (5 * rows, cols + 2 * LANES),
    )
    f32 = jnp.float32
    vmem = pl.BlockSpec(memory_space=pltpu.VMEM)
    smem = pl.BlockSpec(memory_space=pltpu.SMEM)
    return pl.pallas_call(
        functools.partial(kernel, row_tiles, col_tiles),
        out_shape=jax.ShapeDtypeStruct(fields.shape, f32),
        in_specs=[vmem, vmem, smem, smem],
        out_specs=vmem,
        scratch_shapes=[
            pltpu.VMEM((2, channels, levels + 2, rows, cols), f32),
            pltpu.VMEM((channels, levels, rows, cols), f32),
            pltpu.VMEM((3, levels, rows, cols + LANES), f32),
            pltpu.VMEM((3, levels, 2 * rows, cols), f32),
            pltpu.VMEM((levels + 1, rows, cols), f32),
            pltpu.VMEM((levels, rows, cols), f32),
            pltpu.VMEM((levels, rows, cols), f32),
            pltpu.VMEM((2, 2, channels, rows, LANES), f32),
            pltpu.VMEM((2, 2, channels, rows, LANES), f32),
            pltpu.VMEM((2, 2, channels, 2 * levels, cols), f32),
            pltpu.VMEM((2, 2, channels, 2 * levels, cols), f32),
            pltpu.VMEM((2, 2, channels, levels, cols), f32),
            pltpu.VMEM((2, 2, 5, levels, cols), f32),
            pltpu.VMEM((2, 3, levels, rows, cols), f32),
            pltpu.VMEM((2, 2, 5, rows, LANES), f32),
            pltpu.VMEM((2, 2, 2, levels, cols), f32),
            pltpu.VMEM((2, levels, rows, cols), f32),
            pltpu.VMEM((2, 3, levels, rows, cols), f32),
            pltpu.SemaphoreType.DMA((2, 20)),
            pltpu.SemaphoreType.DMA((2, 12)),
        ],
        compiler_params=pltpu.CompilerParams(
            collective_id=0, has_side_effects=True, vmem_limit_bytes=48 * 1024 * 1024
        ),
    )(fields, depth, reaction, growth)


def solution(mesh):
    return jax.shard_map(
        on_device,
        mesh=mesh,
        in_specs=(P("section", None, None, "gy", "gx"), P(), P(), P(), P()),
        out_specs=P("section", None, None, "gy", "gx"),
        check_vma=False,
    )
```

profile of v0, /device:TPU:1, one launch (start us, length us, event | category | flops | bytes accessed | tf_op | source)
XLA Modules:
  0.0 54.8 jit_solution(15116908013665993010)
XLA Ops:
  0.0 1.0 %compare_select_fusion = s32[96,512]{1,0:T(8,128)S(1)} fusion(s32[96,512]{1,0:T(8,128)} %param.7, s32[96,512]{1,0:T(8,128)} %param.6), kind=kLoop, calls=%fused_computation.1 | loop fusion | flops 98304 | bytes 589824 | tf_op jit(solution)/shard_map/jit(_where)/select_n | solution.py:481
  1.1 0.0 copy-start
  1.1 1.5 %copy-done = f32[1,15,16,8,256]{4,3,2,1,0:T(8,128)S(1)} copy-done((f32[1,15,16,8,256]{4,3,2,1,0:T(8,128)S(1)}, f32[1,15,16,8,256]{4,3,2,1,0:T(8,128)}, u32[]{:S(2)}) %copy-start) | copy-done | bytes 1966104
  2.6 0.0 copy-start.1
  2.6 0.7 %copy-done.1 = f32[15,15]{1,0:T(8,128)S(1)} copy-done((f32[15,15]{1,0:T(8,128)S(1)}, f32[15,15]{1,0:T(8,128)}, u32[]{:S(2)}) %copy-start.1) | copy-done | bytes 924
  3.3 0.0 copy-start.2
  3.3 0.7 %copy-done.2 = f32[15]{0:T(128)S(1)} copy-done((f32[15]{0:T(128)S(1)}, f32[15]{0:T(128)}, u32[]{:S(2)}) %copy-start.2) | copy-done | bytes 84
  4.0 49.5 %shard_map.55 = f32[1,15,16,8,256]{4,3,2,1,0:T(8,128)S(1)} custom-call(f32[1,15,16,8,256]{4,3,2,1,0:T(8,128)S(1)} %copy-done, s32[40,512]{1,0:T(8,128)S(1)} %pad_dynamic-slice_fusion.depth, f32[15,15]{1,0:T(8,128)S(1)} %copy-done.1, f32[15]{0:T(128)S(1)} %copy-done.2), custom_call_target="tpu_custom_call" | custom-call | tf_op jit(solution)/shard_map/pallas_call | solution.py:491
  53.5 1.3 %copy.7 = f32[1,15,16,8,256]{4,3,2,1,0:T(8,128)} copy(f32[1,15,16,8,256]{4,3,2,1,0:T(8,128)S(1)} %shard_map.55) | data formatting | bytes 3932160
  (1 shorter events, 0.0 us)
Async XLA Ops:
  1.1 1.5 %copy-start = (f32[1,15,16,8,256]{4,3,2,1,0:T(8,128)S(1)}, f32[1,15,16,8,256]{4,3,2,1,0:T(8,128)}, u32[]{:S(2)}) copy-start(f32[1,15,16,8,256]{4,3,2,1,0:T(8,128)} %fields.1) | copy-start | bytes 5898244
  2.6 0.7 %copy-start.1 = (f32[15,15]{1,0:T(8,128)S(1)}, f32[15,15]{1,0:T(8,128)}, u32[]{:S(2)}) copy-start(f32[15,15]{1,0:T(8,128)} %reaction.1) | copy-start | bytes 2704
  3.3 0.7 %copy-start.2 = (f32[15]{0:T(128)S(1)}, f32[15]{0:T(128)}, u32[]{:S(2)}) copy-start(f32[15]{0:T(128)} %growth.1) | copy-start | bytes 184
where the time goes:
time: 55 us; the launch traced here: 54.8 us
  Pallas kernels  49.5 us (90%)
  local copies, waits for them, and re-layouts  4.19 us (8%)
  other arithmetic  1.05 us (2%)
    pallas_call x1, Pallas kernels, on_device(): pl.pallas_call(functools.partial(kernel, row_tiles, col_tiles), out_shape...  49.5 us
    unnamed x7, local copies, waits for them, and re-layouts  4.17 us

commit v1 on v0

--- a/solution.py
+++ b/solution.py
@@ -29,7 +29,7 @@
 MESH = pl.DeviceIdType.MESH
 LANES = 128
 SUBS = 8
-KB = 4
+KB = 2
 SLOT_FIELD = (0, 1, 4, 2, 3)
 U, V, E, T, S = range(5)
 
@@ -46,17 +46,22 @@
     return pltpu.roll(x, x.shape[axis] - 1, axis)
 
 
+def turned(x, shift):
+    shift %= SUBS
+    return pltpu.roll(x, shift, 0) if shift else x
+
+
 def behind(x, axis):
     return pltpu.roll(x, 1, axis)
 
 
 def kernel(
     row_tiles, col_tiles,
-    fields, depth, reaction, growth, out,
+    fields, depth, reaction_hbm, growth_hbm, out,
     state, base, coef_c, coef_r, coef_v, uptake, sun,
     col_out, col_in, row_out, row_in, orow_out, orow_in,
     flow_in, fcol_in, frow_in, heat_out, heat_in,
-    send_sem, recv_sem,
+    send_sem, recv_sem, load_sem, reaction, growth,
 ):
     channels, levels, rows, cols = fields.shape[1:]
     section = lax.axis_index("section")
@@ -116,18 +121,24 @@
             (has_e, copy(col_out.at[step, 1], col_in.at[step, 0], step, 1, 0, (section, g, x + 1))),
         ]
 
-    def tracer_row_sends(step):
+    part = channels // 3
+
+    def tracer_row_sends(step, j):
+        some = pl.ds(part * j, part)
         return [
-            (has_lo, copy(row_out.at[step, 0], row_in.at[step, 1], step, 2, 3, band_device(jnp.maximum(band - 1, 0)))),
-            (has_hi, copy(row_out.at[step, 1], row_in.at[step, 0], step, 3, 2, band_device(band + 1))),
+            (has_lo, copy(row_out.at[step, 0, some], row_in.at[step, 1, some], step, 20 + j, 15 + j, band_device(jnp.maximum(band - 1, 0)))),
+            (has_hi, copy(row_out.at[step, 1, some], row_in.at[step, 0, some], step, 23 + j, 12 + j, band_device(band + 1))),
         ]
 
     def heat_send(step):
         return copy(heat_out.at[step], heat_in.at[step, third], step, 4, 9 + third, (0, g, x))
 
+    def sent(step):
+        return 2 if step else 3
+
     def flow_sends(step):
         return [
-            (is_ocean, copy(state.at[step, pl.ds(5 * t, 3), pl.ds(1, levels)], flow_in.at[step], step, 5 + t, 4, own_tracer(t, x)))
+            (is_ocean, copy(state.at[step, pl.ds(5 * t, sent(step)), pl.ds(1, levels)], flow_in.at[step, pl.ds(0, sent(step))], step, 5 + t, 4, own_tracer(t, x)))
             for t in range(3)
         ]
 
@@ -222,12 +233,20 @@
         both_r = jnp.minimum(along, along_next)
 
         def load(c, carry):
-            state[0, c, pl.ds(1, levels)] = fields[0, c]
             for slot in range(2):
                 state[slot, c, 0] = jnp.zeros((rows, cols), jnp.float32)
                 state[slot, c, levels + 1] = jnp.zeros((rows, cols), jnp.float32)
             return carry
+        whole = pltpu.make_async_copy(fields.at[0], state.at[0, :, pl.ds(1, levels)], load_sem.at[0])
+        whole.start()
+        tables = [
+            pltpu.make_async_copy(reaction_hbm, reaction, load_sem.at[1]),
+            pltpu.make_async_copy(growth_hbm, growth, load_sem.at[2]),
+        ]
+        for one in tables:
+            one.start()
         lax.fori_loop(0, channels, load, 0)
+        whole.wait()
 
         for step in range(STEPS):
             last = step == STEPS - 1
@@ -237,10 +256,13 @@
                     row_out[step, 0, c, 2 * k:2 * k + 2] = state[step, c, k + 1, 0:2]
                     row_out[step, 1, c, 2 * k:2 * k + 2] = state[step, c, k + 1, rows - 2:rows]
                 return carry
-            lax.fori_loop(0, channels, pack_rows, 0)
             if step == 0:
+                lax.fori_loop(0, channels, pack_rows, 0)
                 pl.semaphore_wait(barrier, count)
-            start(tracer_row_sends(step))
+                for j in range(3):
+                    start(tracer_row_sends(step, j))
+            pack_columns(step)
+            start(common_sends(step))
             optical = jnp.zeros((rows, cols), jnp.float32)
             for k in range(levels):
                 chlorophyll = jnp.maximum(state[step, 2, k + 1], 0.0)
@@ -250,8 +272,9 @@
                 nutrient = jnp.maximum(state[step, 0, k + 1], 0.0)
                 uptake[k] = nutrient / (nutrient + HALF_SAT) * light * TIME_INCREMENT
             heat_send(step).start()
-            pack_columns(step)
-            start(common_sends(step))
+            if step == 0:
+                for one in tables:
+                    one.wait()
 
             def react(k, carry):
                 values = [state[step, c, k + 1] for c in range(channels)]
@@ -266,7 +289,17 @@
                 return carry
             lax.fori_loop(0, levels, react, 0)
 
-            arrived(is_tracer, flow_in.at[step], step, 4)
+            arrived(is_tracer, flow_in.at[step, pl.ds(0, sent(step))], step, 4)
+            if step:
+                for k in range(levels):
+                    energy = flow_in[step - 1, E, k]
+                    shear = jnp.zeros((rows, cols), jnp.float32)
+                    if k < levels - 1:
+                        du = flow_in[step - 1, U, k + 1] - flow_in[step - 1, U, k]
+                        dv = flow_in[step - 1, V, k + 1] - flow_in[step - 1, V, k]
+                        shear = jnp.where(k + 1 < middle, du * du + dv * dv, 0.0)
+                    flow_in[step, E, k] = jnp.where(k < middle, energy + TIME_INCREMENT * (
+                        SHEAR_GAIN * shear - DISSIPATION * energy), 0.0)
             arrived(has_w, fcol_in.at[step, 0], step, 5)
             arrived(has_e, fcol_in.at[step, 1], step, 6)
             arrived(has_lo, frow_in.at[step, 0], step, 7)
@@ -302,8 +335,6 @@
 
             arrived(has_w, col_in.at[step, 0], step, 0)
             arrived(has_e, col_in.at[step, 1], step, 1)
-            arrived(has_lo, row_in.at[step, 0], step, 2)
-            arrived(has_hi, row_in.at[step, 1], step, 3)
 
             def fluxes(q, coefs, k0, axis):
                 window = pl.ds(k0, KB)
@@ -316,27 +347,35 @@
                 )
                 return behind(flux, axis) - flux
 
-            def advance(c, carry):
+            def advance_columns(c, carry):
                 low_c, high_c = col_in[step, 0, c], col_in[step, 1, c]
                 for k0 in range(0, levels, KB):
                     q = state[step, c, pl.ds(k0 + 1, KB)]
                     halo = jnp.stack([column_halo(low_c, high_c, k0 + j) for j in range(KB)])
                     total = base[c, pl.ds(k0, KB)]
                     total = total + fluxes(jnp.concatenate([q, halo], axis=2), coef_c, k0, 2)[:, :, :cols]
-                    low_r = row_in[step, 0, c, pl.ds(2 * k0, 2 * KB)]
-                    high_r = row_in[step, 1, c, pl.ds(2 * k0, 2 * KB)]
+                    up = coef_v[pl.ds(k0 + 1, KB)] * (state[step, c, pl.ds(k0 + 2, KB)] - q)
+                    down = coef_v[pl.ds(k0, KB)] * (q - state[step, c, pl.ds(k0, KB)])
+                    base[c, pl.ds(k0, KB)] = total + (up - down)
+                return carry
+            lax.fori_loop(0, channels, advance_columns, 0)
+
+            def advance_rows(c, carry):
+                for k0 in range(0, levels, KB):
+                    q = state[step, c, pl.ds(k0 + 1, KB)]
+                    total = base[c, pl.ds(k0, KB)]
+                    first = 2 * k0 % SUBS
+                    low_r = row_in[step, 0, c, pl.ds(2 * k0 - first, SUBS)]
+                    high_r = row_in[step, 1, c, pl.ds(2 * k0 - first, SUBS)]
                     halo = jnp.stack([
                         jnp.where(
                             sub_full < SUBS // 2,
-                            pltpu.roll(high_r, SUBS - 2 * j, 0) if j else high_r,
-                            pltpu.roll(low_r, SUBS - 2 - 2 * j, 0) if j < KB - 1 else low_r,
+                            turned(high_r, -first - 2 * j),
+                            turned(low_r, -2 - first - 2 * j),
                         )
                         for j in range(KB)
                     ])
                     total = total + fluxes(jnp.concatenate([q, halo], axis=1), coef_r, k0, 1)[:, :rows]
-                    up = coef_v[pl.ds(k0 + 1, KB)] * (state[step, c, pl.ds(k0 + 2, KB)] - q)
-                    down = coef_v[pl.ds(k0, KB)] * (q - state[step, c, pl.ds(k0, KB)])
-                    total = total + (up - down)
                     fresh = jnp.stack([
                         jnp.where(k0 + j < middle, total[j], 0.0) for j in range(KB)
                     ])
@@ -344,21 +383,45 @@
                         out[0, c, pl.ds(k0, KB)] = fresh
                     else:
                         state[step + 1, c, pl.ds(k0 + 1, KB)] = fresh
-                return carry
-            lax.fori_loop(0, channels, advance, 0)
+                        for j in range(KB):
+                            two = slice(2 * (k0 + j), 2 * (k0 + j) + 2)
+                            row_out[step + 1, 0, c, two] = fresh[j, 0:2]
+                            row_out[step + 1, 1, c, two] = fresh[j, rows - 2:rows]
+                return carry
+            for j in range(3):
+                some = pl.ds(part * j, part)
+                arrived(has_lo, row_in.at[step, 0, some], step, 12 + j)
+                arrived(has_hi, row_in.at[step, 1, some], step, 15 + j)
+                lax.fori_loop(part * j, part * (j + 1), advance_rows, 0)
+                if not last:
+                    start(tracer_row_sends(step + 1, j))
 
         for step in range(STEPS):
-            finish(tracer_row_sends(step) + common_sends(step))
+            finish(common_sends(step))
+            for j in range(3):
+                finish(tracer_row_sends(step, j))
             heat_send(step).wait_send()
 
     def ocean():
+        loads = [
+            pltpu.make_async_copy(
+                fields.at[0, 3 * SLOT_FIELD[slot] + t],
+                state.at[0, 5 * t + slot, pl.ds(1, levels)],
+                load_sem.at[5 * t + slot],
+            )
+            for t in range(3) for slot in range(5)
+        ]
+        for one in loads:
+            one.start()
+
         def load(t, carry):
             for slot in range(5):
-                state[0, 5 * t + slot, pl.ds(1, levels)] = fields[0, 3 * SLOT_FIELD[slot] + t]
                 for step in range(2):
                     state[step, 5 * t + slot, levels + 1] = jnp.zeros((rows, cols), jnp.float32)
             return carry
         lax.fori_loop(0, 3, load, 0)
+        for one in loads:
+            one.wait()
         views = []
         for t in range(3):
             middle, across, along = depth_views(t)
@@ -487,11 +550,11 @@
     )
     f32 = jnp.float32
     vmem = pl.BlockSpec(memory_space=pltpu.VMEM)
-    smem = pl.BlockSpec(memory_space=pltpu.SMEM)
+    whole = pl.BlockSpec(memory_space=pltpu.HBM)
     return pl.pallas_call(
         functools.partial(kernel, row_tiles, col_tiles),
         out_shape=jax.ShapeDtypeStruct(fields.shape, f32),
-        in_specs=[vmem, vmem, smem, smem],
+        in_specs=[whole, vmem, whole, whole],
         out_specs=vmem,
         scratch_shapes=[
             pltpu.VMEM((2, channels, levels + 2, rows, cols), f32),
@@ -512,8 +575,11 @@
             pltpu.VMEM((2, 2, 2, levels, cols), f32),
             pltpu.VMEM((2, levels, rows, cols), f32),
             pltpu.VMEM((2, 3, levels, rows, cols), f32),
-            pltpu.SemaphoreType.DMA((2, 20)),
-            pltpu.SemaphoreType.DMA((2, 12)),
+            pltpu.SemaphoreType.DMA((2, 26)),
+            pltpu.SemaphoreType.DMA((2, 18)),
+            pltpu.SemaphoreType.DMA((15,)),
+            pltpu.SMEM(reaction.shape, f32),
+            pltpu.SMEM(growth.shape, f32),
         ],
         compiler_params=pltpu.CompilerParams(
             collective_id=0, has_side_effects=True, vmem_limit_bytes=48 * 1024 * 1024

time: 55 us -> 53.6 us (0.975)
  the two profiles are of different devices: /device:TPU:1 before, /device:TPU:4 now
where the time goes in v1:
time: 53.6 us; the launch traced here: 53.4 us
  Pallas kernels  48.1 us (90%)
  local copies, waits for them, and re-layouts  4.19 us (8%)
  other arithmetic  1.05 us (2%)
    pallas_call x1, Pallas kernels, on_device(): pl.pallas_call(functools.partial(kernel, row_tiles, col_tiles), out_shape...  48.1 us
    unnamed x7, local copies, waits for them, and re-layouts  4.17 us

profile of v1, /device:TPU:4, one launch (start us, length us, event | category | flops | bytes accessed | tf_op | source)
XLA Modules:
  0.0 53.4 jit_solution(5691119415168751324)
XLA Ops:
  0.0 1.0 %compare_select_fusion = s32[96,512]{1,0:T(8,128)S(1)} fusion(s32[96,512]{1,0:T(8,128)} %param.7, s32[96,512]{1,0:T(8,128)} %param.6), kind=kLoop, calls=%fused_computation.1 | loop fusion | flops 98304 | bytes 589824 | tf_op jit(solution)/shard_map/jit(_where)/select_n | solution.py:544
  1.1 0.0 copy-start
  1.1 1.5 %copy-done = f32[1,15,16,8,256]{4,3,2,1,0:T(8,128)S(1)} copy-done((f32[1,15,16,8,256]{4,3,2,1,0:T(8,128)S(1)}, f32[1,15,16,8,256]{4,3,2,1,0:T(8,128)}, u32[]{:S(2)}) %copy-start) | copy-done | bytes 1966104
  2.6 0.0 copy-start.1
  2.6 0.7 %copy-done.1 = f32[15,15]{1,0:T(8,128)S(1)} copy-done((f32[15,15]{1,0:T(8,128)S(1)}, f32[15,15]{1,0:T(8,128)}, u32[]{:S(2)}) %copy-start.1) | copy-done | bytes 924
  3.3 0.0 copy-start.2
  3.3 0.7 %copy-done.2 = f32[15]{0:T(128)S(1)} copy-done((f32[15]{0:T(128)S(1)}, f32[15]{0:T(128)}, u32[]{:S(2)}) %copy-start.2) | copy-done | bytes 84
  4.0 48.1 %shard_map.55 = f32[1,15,16,8,256]{4,3,2,1,0:T(8,128)S(1)} custom-call(f32[1,15,16,8,256]{4,3,2,1,0:T(8,128)S(1)} %copy-done, s32[40,512]{1,0:T(8,128)S(1)} %pad_dynamic-slice_fusion.depth, f32[15,15]{1,0:T(8,128)S(1)} %copy-done.1, f32[15]{0:T(128)S(1)} %copy-done.2), custom_call_target="tpu_custom_call" | custom-call | tf_op jit(solution)/shard_map/pallas_call | solution.py:554
  52.1 1.3 %copy.7 = f32[1,15,16,8,256]{4,3,2,1,0:T(8,128)} copy(f32[1,15,16,8,256]{4,3,2,1,0:T(8,128)S(1)} %shard_map.55) | data formatting | bytes 3932160
  (1 shorter events, 0.0 us)
Async XLA Ops:
  1.1 1.5 %copy-start = (f32[1,15,16,8,256]{4,3,2,1,0:T(8,128)S(1)}, f32[1,15,16,8,256]{4,3,2,1,0:T(8,128)}, u32[]{:S(2)}) copy-start(f32[1,15,16,8,256]{4,3,2,1,0:T(8,128)} %fields.1) | copy-start | bytes 5898244
  2.6 0.7 %copy-start.1 = (f32[15,15]{1,0:T(8,128)S(1)}, f32[15,15]{1,0:T(8,128)}, u32[]{:S(2)}) copy-start(f32[15,15]{1,0:T(8,128)} %reaction_hbm.1) | copy-start | bytes 2704
  3.3 0.7 %copy-start.2 = (f32[15]{0:T(128)S(1)}, f32[15]{0:T(128)}, u32[]{:S(2)}) copy-start(f32[15]{0:T(128)} %growth_hbm.1) | copy-start | bytes 184
